TPU v7x, 32 devices: a whole 2x2x4 slice. The times are simulated.
32 devices in a mesh: row: 8 (over y, x, core), col: 4 (over z).
Axes of the slice: x: 2, y: 2, z: 4, core: 2. Of those that a mesh axis runs over, the one named last changes fastest.
Arguments:
- embeddings: bfloat16 [4096, 256], P(('row', 'col')), may hold values from -6 to 6
- cotangent: bfloat16 [4096, 256], P(('row', 'col')), may hold values from -6 to 6
- weight: bfloat16 [256, 256], replicated, may hold values from -0.375 to 0.375
- tiles: bfloat16 [32, 128, 128, 128], P(('row', 'col')), may hold values from -0.078125 to 0.078125
- tile_dst: int32 [32, 128], P(('row', 'col')), may hold values from 0 to 3
- tile_src: int32 [32, 128], P(('row', 'col')), may hold values from 0 to 7
- tile_count: int32 [32], P(('row', 'col')), may hold values from 1 to 128, as said below
Outputs:
- output: bfloat16 [4096, 256], P(('row', 'col'))
- grad_embeddings: bfloat16 [4096, 256], P(('row', 'col'))
- grad_weight: float32 [256, 256], replicated
Inputs may be any that keep to these rules, and one draw needn't show every extreme that they name: `tile_count`: at least one device has exactly 128 live slots.
All inputs are finite; a program needn't handle non-finite values.
Results may differ from a plain program's by a relative error of at most 0.012.
Values may be sent and summed in bfloat16 or wider, within the bound.
A program may use at most 128 MiB of HBM per device.

v0:
```python
import math
import jax
import jax.numpy as jnp
from jax import lax
from jax.sharding import PartitionSpec as P


def shards(embeddings, cotangent, weight, tiles, tile_dst, tile_src, tile_count):
    highest = lax.Precision.HIGHEST
    block_rows = embeddings.shape[0]
    feature_width = embeddings.shape[1]
    row_count = lax.axis_size("row")
    column_count = lax.axis_size("col")
    local_tiles = tiles[0]
    dest_ids = tile_dst[0]
    source_ids = tile_src[0]
    slot_ids = jnp.arange(local_tiles.shape[0], dtype=jnp.int32)
    alive_slots = (slot_ids < tile_count[0]).astype(jnp.float32)
    dest_onehot = (dest_ids[:, None] == jnp.arange(column_count, dtype=jnp.int32)[None, :]).astype(
        jnp.float32
    ) * alive_slots[:, None]
    source_onehot = (source_ids[:, None] == jnp.arange(row_count, dtype=jnp.int32)[None, :]).astype(
        jnp.float32
    ) * alive_slots[:, None]
    gathered = lax.all_gather(embeddings, "row", axis=0, tiled=True).reshape(
        row_count, block_rows, feature_width
    )
    chosen = jnp.take(gathered, source_ids, axis=0)
    products = jnp.einsum("tij,tjd->tid", local_tiles, chosen, preferred_element_type=jnp.float32)
    partial_value = jnp.einsum("tc,tid->cid", dest_onehot, products, precision=highest)
    partial_rounded = partial_value.astype(jnp.bfloat16).reshape(
        column_count * block_rows, feature_width
    )
    summed = lax.psum_scatter(
        partial_rounded.astype(jnp.float32).astype(jnp.bfloat16),
        "col",
        scatter_dimension=0,
        tiled=True,
    ).astype(jnp.float32)
    hidden = summed.astype(jnp.bfloat16)
    output = jnp.dot(hidden, weight, preferred_element_type=jnp.float32).astype(jnp.bfloat16)
    user_count = block_rows * row_count * column_count
    scale_factor = 1.0 / math.sqrt(user_count)
    contract_rows = (((0,), (0,)), ((), ()))
    contract_cols = (((1,), (1,)), ((), ()))
    grad_hidden = lax.dot_general(
        cotangent, weight, contract_cols, preferred_element_type=jnp.float32
    ).astype(jnp.bfloat16)
    grad_group = lax.all_gather(grad_hidden, "col", axis=0, tiled=True)
    weight_term = lax.dot_general(
        summed, cotangent.astype(jnp.float32), contract_rows, precision=highest
    )
    grad_weight = lax.psum(weight_term, ("row", "col")) * scale_factor
    dest_rows = grad_group.reshape(column_count, block_rows, feature_width)
    picked = jnp.take(dest_rows, dest_ids, axis=0)
    back_products = jnp.einsum(
        "tji,tjd->tid", local_tiles, picked, preferred_element_type=jnp.float32
    )
    back_partial = jnp.einsum("tr,tid->rid", source_onehot, back_products, precision=highest)
    back_rounded = lax.optimization_barrier(back_partial.astype(jnp.bfloat16)).astype(jnp.float32)
    back_summed = lax.psum_scatter(
        back_rounded.reshape(row_count * block_rows, feature_width).astype(jnp.bfloat16),
        "row",
        scatter_dimension=0,
        tiled=True,
    )
    return (output, back_summed, grad_weight)


def solution(mesh):
    in_specs = (
        P(("row", "col"), None),
        P(("row", "col"), None),
        P(),
        P(("row", "col"), None, None, None),
        P(("row", "col"), None),
        P(("row", "col"), None),
        P(("row", "col")),
    )
    out_specs = (P(("row", "col"), None), P(("row", "col"), None), P())
    return jax.shard_map(shards, mesh=mesh, in_specs=in_specs, out_specs=out_specs, check_vma=False)
```

profile of v0, /device:TPU:0, one launch (start us, length us, event | category | flops | bytes accessed | tf_op | source)
XLA Modules:
  0.0 260.4 jit_solution(8117860961400061152)
XLA Ops:
  8.0 0.0 copy-start
  8.0 0.0 reduce-scatter.3.cloned.1.call-start
  8.1 0.7 fusion.30
  8.7 0.7 compare_and_fusion.1
  9.4 11.6 %all_gather.6 = bf16[1024,256]{1,0:T(8,128)(2,1)S(1)} all-gather(bf16[128,256]{1,0:T(8,128)(2,1)} %param.7), channel_id=1, replica_groups=mesh['row'=8,'col'=4] {'row'}, dimensions={0}, use_global_device_ids=true | all-gather | bytes 589824 | tf_op jit(solution)/shard_map/all_gather | solution.py:25
  21.0 6.5 %gather_fusion = bf16[128,128,256]{2,1,0:T(8,128)(2,1)} fusion(bf16[8,128,256]{2,1,0:T(8,128)(2,1)S(1)} %bitcast.46, s32[1024]{0:T(1024)S(1)} %pad_clamp_fusion.1), kind=kCustom, calls=%fused_computation | custom fusion | bytes 16777728 | tf_op jit(solution)/shard_map/jit(_take)/gather | solution.py:28
  27.5 13.1 %fusion.6 = f32[128,256,128]{2,1,0:T(8,128)} fusion(bf16[128,128,256]{2,1,0:T(8,128)(2,1)} %gather_fusion, pred[128]{0:T(512)(128)(4,1)S(1)} %compare_and_fusion.1, bf16[1,128,128,128]{3,2,1,0:T(8,128)(2,1)} %param.10), kind=kOutput, calls=%fused_computation.8 | convolution fusion | flops 1077936128 | bytes 29360256 | tf_op jit(solution)/shard_map/tij,tjd->tid/dot_general | solution.py:29
  40.6 17.7 %copy.12 = f32[128,256,128]{1,0,2:T(8,128)} copy(f32[128,256,128]{2,1,0:T(8,128)} %fusion.6) | data formatting | bytes 33554432 | tf_op jit(solution)/shard_map/tij,tjd->tid/dot_general | solution.py:29
  59.0 0.0 copy-done.3
  59.0 0.0 copy-start.1
  59.0 10.8 %fusion.17 = bf16[4,128,256]{2,0,1:T(4,128)(2,1)S(1)} fusion(f32[128,256,128]{1,0,2:T(8,128)} %copy.12, f32[128]{0:T(128)S(1)} %compare_convert_fusion, s32[128]{0:T(128)S(1)} %bitcast.49), kind=kOutput, calls=%fused_computation.17 | convolution fusion | flops 201458688 | bytes 17040384 | tf_op jit(solution)/shard_map/tc,tid->cid/dot_general | solution.py:30
  69.8 0.7 copy.10
  70.6 0.0 reduce-scatter.3.cloned.1.call-update
  70.6 0.0 all-reduce.2.cloned.1.call-start
  70.7 0.0 copy-done
  70.7 0.0 copy-done.1
  70.7 0.2 convolution_convert_fusion
  70.9 15.5 %all_gather.7 = bf16[512,256]{1,0:T(8,128)(2,1)S(1)} all-gather(bf16[128,256]{1,0:T(8,128)(2,1)S(1)} %convolution_convert_fusion), channel_id=1, replica_groups=mesh['row'=8,'col'=4] {'col'}, dimensions={0}, use_global_device_ids=true | all-gather | bytes 327680 | tf_op jit(solution)/shard_map/all_gather | solution.py:49
  86.4 6.5 %gather_fusion.1 = bf16[128,128,256]{2,1,0:T(8,128)(2,1)} fusion(bf16[4,128,256]{2,1,0:T(8,128)(2,1)S(1)} %bitcast.45, s32[1024]{0:T(1024)S(1)} %pad_clamp_fusion), kind=kCustom, calls=%fused_computation.1 | custom fusion | bytes 16777728 | tf_op jit(solution)/shard_map/jit(_take)/gather | solution.py:55
  92.9 12.8 %fusion.4 = f32[128,256,128]{2,1,0:T(8,128)} fusion(bf16[128,128,256]{2,1,0:T(8,128)(2,1)} %gather_fusion.1, pred[128]{0:T(512)(128)(4,1)S(1)} %compare_and_fusion, bf16[1,128,128,128]{3,2,1,0:T(8,128)(2,1)} %param.10), kind=kOutput, calls=%fused_computation.6 | convolution fusion | flops 1077936128 | bytes 29360256 | tf_op jit(solution)/shard_map/tji,tjd->tid/dot_general | solution.py:56
  105.7 17.7 %copy.13 = f32[128,256,128]{1,0,2:T(8,128)} copy(f32[128,256,128]{2,1,0:T(8,128)} %fusion.4) | data formatting | bytes 33554432 | tf_op jit(solution)/shard_map/tji,tjd->tid/dot_general | solution.py:56
  123.4 1.7 fusion.36
  125.1 0.0 all-reduce.2.cloned.1.call-update
  125.2 0.0 reduce-scatter.5.cloned.1.call-start
  125.2 0.0 copy-done.4
  125.2 0.0 copy-start.2
  125.2 10.8 %fusion.14 = bf16[8,128,256]{2,0,1:T(8,128)(2,1)S(1)} fusion(f32[128,256,128]{1,0,2:T(8,128)} %copy.13, f32[128]{0:T(128)S(1)} %compare_convert_fusion, s32[128]{0:T(128)S(1)} %bitcast.50), kind=kOutput, calls=%fused_computation.16 | convolution fusion | flops 402917376 | bytes 17302528 | tf_op jit(solution)/shard_map/tr,tid->rid/dot_general | solution.py:59
  136.1 0.9 copy.11
  137.0 0.0 reduce-scatter.5.cloned.1.call-update
  137.0 0.8 convolution_convert_fusion.1
  137.8 113.4 %all-reduce.2.cloned.1.call-done = f32[256,256]{1,0:T(8,128)} async-done(((f32[256,256]{1,0:T(8,128)}), f32[256,256]{1,0:T(8,128)}) %all-reduce.2.cloned.1.call-update) | async-done | bytes 262160 | tf_op jit(solution)/shard_map/psum | solution.py:53
  251.3 1.7 broadcast_multiply_fusion
  (10 shorter events, 0.0 us)
Async XLA Ops:
  8.0 62.7 %copy-start = (bf16[256,256]{1,0:T(8,128)(2,1)S(1)}, bf16[256,256]{1,0:T(8,128)(2,1)}, u32[]{:S(2)}) copy-start(bf16[256,256]{1,0:T(8,128)(2,1)} %param.9) | copy-start | bytes 393220
  8.0 115.4 %reduce-scatter.3.cloned.1.call-start = ((), (), s32[]{:S(2)}) async-start(), calls=%async_computation.2 | async-start | bytes 327680 | tf_op jit(solution)/shard_map/reduce_scatter | solution.py:34
  40.6 18.4 %copy-start.3 = (s32[1,128]{1,0:T(1,128)S(1)}, s32[1,128]{1,0:T(1,128)}, u32[]{:S(2)}) copy-start(s32[1,128]{1,0:T(1,128)} %param.11) | copy-start | bytes 1540
  59.0 11.7 %copy-start.1 = (bf16[128,256]{1,0:T(8,128)(2,1)S(1)}, bf16[128,256]{1,0:T(8,128)(2,1)}, u32[]{:S(2)}) copy-start(bf16[128,256]{1,0:T(8,128)(2,1)} %param.8) | copy-start | bytes 196612
  70.6 180.7 %all-reduce.2.cloned.1.call-start = ((), (), s32[]{:S(2)}) async-start(), calls=%async_computation.4 | async-start | bytes 524288 | tf_op jit(solution)/shard_map/psum | solution.py:53
  105.7 19.5 %copy-start.4 = (s32[1,128]{1,0:T(1,128)S(1)}, s32[1,128]{1,0:T(1,128)}, u32[]{:S(2)}) copy-start(s32[1,128]{1,0:T(1,128)} %param.12) | copy-start | bytes 1540
  125.2 127.8 %reduce-scatter.5.cloned.1.call-start = ((), (), s32[]{:S(2)}) async-start(), calls=%async_computation.3 | async-start | bytes 589824 | tf_op jit(solution)/shard_map/reduce_scatter | solution.py:61
  125.2 11.8 %copy-start.2 = (bf16[128,256]{1,0:T(8,128)(2,1)S(1)}, bf16[128,256]{1,0:T(8,128)(2,1)}, u32[]{:S(2)}) copy-start(bf16[128,256]{1,0:T(8,128)(2,1)} %reduce-scatter.3.cloned.1.call-done) | copy-start | bytes 196612
Sparse Core Ops, SparseCore 0:
  70.7 20.6 reduce-scatter.2
  125.3 125.9 all-reduce.1
Sparse Core Ops, SparseCore 1:
  137.1 34.8 reduce-scatter.4
where the time goes:
time: 261 us; the launch traced here: 260 us
  waiting for transfers between devices  113 us (43%)
  matrix products  50.3 us (19%)
  local copies, waits for them, and re-layouts  50 us (19%)
  blocking collectives  27.1 us (10%)
  between operations  16.3 us (6%)
  other arithmetic  3.05 us (1%)
    psum x1, waiting for transfers between devices, shards(): grad_weight = lax.psum(weight_term, ('row', 'col')) * scale_factor  113 us
    dot_general x1, local copies, waits for them, and re-layouts, shards(): jnp.einsum('tij,tjd->tid', local_tiles, chosen, preferred_element_type=jn...  17.7 us
    dot_general x1, local copies, waits for them, and re-layouts, shards(): jnp.einsum('tji,tjd->tid', local_tiles, picked, preferred_element_type=jn...  17.7 us
    all_gather x1, blocking collectives, shards(): grad_group = lax.all_gather(grad_hidden, 'col', axis=0, tiled=True)  15.5 us
    dot_general x1, matrix products, shards(): jnp.einsum('tij,tjd->tid', local_tiles, chosen, preferred_element_type=jn...  13.1 us
    dot_general x1, matrix products, shards(): jnp.einsum('tji,tjd->tid', local_tiles, picked, preferred_element_type=jn...  12.8 us
    all_gather x1, blocking collectives, shards(): lax.all_gather(embeddings, 'row', axis=0, tiled=True)  11.6 us
    dot_general x1, matrix products, shards(): jnp.einsum('tc,tid->cid', dest_onehot, products, precision=highest)  10.8 us
  transfers between devices with their start and end apart: 3, of which 1 were waited for; matrix products, arithmetic and copies ran while one was open for 20% of the time, Pallas kernels for 0%

commit v1 on v0

--- a/solution.py
+++ b/solution.py
@@ -46,7 +46,12 @@
     grad_hidden = lax.dot_general(
         cotangent, weight, contract_cols, preferred_element_type=jnp.float32
     ).astype(jnp.bfloat16)
-    grad_group = lax.all_gather(grad_hidden, "col", axis=0, tiled=True)
+    ring = [grad_hidden]
+    for hop in range(3):
+        ring.append(lax.ppermute(ring[-1], "col", [(dev, (dev + 1) % 4) for dev in range(4)]))
+    grad_group = jnp.roll(
+        jnp.concatenate(ring[::-1], axis=0), (lax.axis_index("col") + 1) * ring[0].shape[0], axis=0
+    )
     weight_term = lax.dot_general(
         summed, cotangent.astype(jnp.float32), contract_rows, precision=highest
     )

time: 261 us -> 259 us (level)
  blocking collectives: 27.1 us -> 10.2 us
  waiting for transfers between devices: 113 us -> 122 us
  starting transfers between devices: 0.12 us -> 4.87 us
    all_gather x1 -> x0, blocking collectives: 15.5 us -> none  [shards(): grad_group = lax.all_gather(grad_hidden, 'col', axis=0, tiled=True)]
    ppermute x0 -> x3, waiting for transfers between devices: none -> 11.5 us  [shards(): lax.ppermute(ring[-1], 'col', [(dev, (dev + 1) % 4) for dev in range(4)])]
    ppermute x0 -> x3, starting transfers between devices: none -> 4.75 us  [shards(): lax.ppermute(ring[-1], 'col', [(dev, (dev + 1) % 4) for dev in range(4)])]
    psum x1, waiting for transfers between devices: 113 us -> 110 us  [shards(): grad_weight = lax.psum(weight_term, ('row', 'col')) * scale_factor]
  transfers between devices with their start and end apart: 3 -> 6, of which waited for: 1 -> 3; matrix products, arithmetic and copies ran while one was open for 20% -> 39% of each run, Pallas kernels for 0% -> 0%
where the time goes in v1:
time: 259 us; the launch traced here: 258 us
  waiting for transfers between devices  122 us (47%)
  matrix products  51.3 us (20%)
  local copies, waits for them, and re-layouts  51.1 us (20%)
  between operations  16.3 us (6%)
  blocking collectives  10.2 us (4%)
  starting transfers between devices  4.87 us (2%)
  other arithmetic  3.01 us (1%)
    psum x1, waiting for transfers between devices, shards(): grad_weight = lax.psum(weight_term, ('row', 'col')) * scale_factor  110 us
    dot_general x1, local copies, waits for them, and re-layouts, shards(): jnp.einsum('tji,tjd->tid', local_tiles, picked, preferred_element_type=jn...  17.7 us
    dot_general x1, local copies, waits for them, and re-layouts, shards(): jnp.einsum('tij,tjd->tid', local_tiles, chosen, preferred_element_type=jn...  17.7 us
    dot_general x1, matrix products, shards(): jnp.einsum('tij,tjd->tid', local_tiles, chosen, preferred_element_type=jn...  13.2 us
    dot_general x1, matrix products, shards(): jnp.einsum('tji,tjd->tid', local_tiles, picked, preferred_element_type=jn...  12.8 us
    ppermute x3, waiting for transfers between devices, shards(): lax.ppermute(ring[-1], 'col', [(dev, (dev + 1) % 4) for dev in range(4)])  11.5 us
    dot_general x1, matrix products, shards(): jnp.einsum('tr,tid->rid', source_onehot, back_products, precision=highest)  10.8 us
    dot_general x1, matrix products, shards(): jnp.einsum('tc,tid->cid', dest_onehot, products, precision=highest)  10.8 us
  transfers between devices with their start and end apart: 6, of which 3 were waited for; matrix products, arithmetic and copies ran while one was open for 39% of the time, Pallas kernels for 0%

profile of v1, /device:TPU:0, one launch (start us, length us, event | category | flops | bytes accessed | tf_op | source)
XLA Modules:
  0.0 258.4 jit_solution(18061226589122918239)
XLA Ops:
  8.0 0.0 copy-start
  8.0 0.0 reduce-scatter.3.cloned.1.call-start
  8.1 0.8 copy-done
  8.9 1.0 convolution_convert_fusion
  9.9 3.1 %collective-permute-start = (bf16[128,256]{1,0:T(8,128)(2,1)S(1)}, bf16[128,256]{1,0:T(8,128)(2,1)S(1)}, u32[]{:S(2)}, u32[]{:S(2)}) collective-permute-start(bf16[128,256]{1,0:T(8,128)(2,1)S(1)} %convolution_convert_fusion), channel_id=1, source_target_pairs={{0,1},{1,2},{2,3},{3,0},{4,5},{5,6},{6,7},{7,4},{8,9},{9,10},{10,1... | collective-permute-start | bytes 196616 | tf_op jit(solution)/shard_map/ppermute | solution.py:51
  13.0 0.7 fusion.30
  13.7 0.7 compare_and_fusion.1
  15.0 10.2 %all_gather.3 = bf16[1024,256]{1,0:T(8,128)(2,1)S(1)} all-gather(bf16[128,256]{1,0:T(8,128)(2,1)} %param.7), channel_id=1, replica_groups=mesh['row'=8,'col'=4] {'row'}, dimensions={0}, use_global_device_ids=true | all-gather | bytes 589824 | tf_op jit(solution)/shard_map/all_gather | solution.py:25
  25.2 6.5 %gather_fusion = bf16[128,128,256]{2,1,0:T(8,128)(2,1)} fusion(bf16[8,128,256]{2,1,0:T(8,128)(2,1)S(1)} %bitcast.46, s32[1024]{0:T(1024)S(1)} %pad_clamp_fusion.1), kind=kCustom, calls=%fused_computation | custom fusion | bytes 16777728 | tf_op jit(solution)/shard_map/jit(_take)/gather | solution.py:28
  31.7 13.2 %fusion.6 = f32[128,256,128]{2,1,0:T(8,128)} fusion(bf16[128,128,256]{2,1,0:T(8,128)(2,1)} %gather_fusion, pred[128]{0:T(512)(128)(4,1)S(1)} %compare_and_fusion.1, bf16[1,128,128,128]{3,2,1,0:T(8,128)(2,1)} %param.10), kind=kOutput, calls=%fused_computation.8 | convolution fusion | flops 1077936128 | bytes 29360256 | tf_op jit(solution)/shard_map/tij,tjd->tid/dot_general | solution.py:29
  44.9 17.7 %copy.12 = f32[128,256,128]{1,0,2:T(8,128)} copy(f32[128,256,128]{2,1,0:T(8,128)} %fusion.6) | data formatting | bytes 33554432 | tf_op jit(solution)/shard_map/tij,tjd->tid/dot_general | solution.py:29
  62.6 10.8 %fusion.17 = bf16[4,128,256]{2,0,1:T(4,128)(2,1)S(1)} fusion(f32[128,256,128]{1,0,2:T(8,128)} %copy.12, f32[128]{0:T(128)S(1)} %compare_convert_fusion, s32[128]{0:T(128)S(1)} %bitcast.49), kind=kOutput, calls=%fused_computation.17 | convolution fusion | flops 201458688 | bytes 17040384 | tf_op jit(solution)/shard_map/tc,tid->cid/dot_general | solution.py:30
  73.4 0.7 copy.10
  74.2 0.0 reduce-scatter.3.cloned.1.call-update
  74.2 0.0 all-reduce.2.cloned.1.call-start
  74.2 0.0 collective-permute-done
  74.2 1.7 collective-permute-start.1
  75.9 4.6 %collective-permute-done.1 = bf16[128,256]{1,0:T(8,128)(2,1)S(1)} collective-permute-done((bf16[128,256]{1,0:T(8,128)(2,1)S(1)}, bf16[128,256]{1,0:T(8,128)(2,1)S(1)}, u32[]{:S(2)}, u32[]{:S(2)}) %collective-permute-start.1) | collective-permute-done | bytes 65568 | tf_op jit(solution)/shard_map/ppermute | solution.py:51
  80.5 0.0 collective-permute-start.2
  80.5 7.0 %collective-permute-done.2 = bf16[128,256]{1,0:T(8,128)(2,1)S(1)} collective-permute-done((bf16[128,256]{1,0:T(8,128)(2,1)S(1)}, bf16[128,256]{1,0:T(8,128)(2,1)S(1)}, u32[]{:S(2)}, u32[]{:S(2)}) %collective-permute-start.2) | collective-permute-done | bytes 65568 | tf_op jit(solution)/shard_map/ppermute | solution.py:51
  87.6 6.5 %gather_fusion.1 = bf16[128,128,256]{2,1,0:T(8,128)(2,1)} fusion(bf16[4,128,256]{2,1,0:T(8,128)(2,1)S(1)} %bitcast.45, s32[1024]{0:T(1024)S(1)} %pad_clamp_fusion), kind=kCustom, calls=%fused_computation.1 | custom fusion | bytes 16777728 | tf_op jit(solution)/shard_map/jit(_take)/gather | solution.py:60
  94.1 12.8 %fusion.4 = f32[128,256,128]{2,1,0:T(8,128)} fusion(bf16[128,128,256]{2,1,0:T(8,128)(2,1)} %gather_fusion.1, pred[128]{0:T(512)(128)(4,1)S(1)} %compare_and_fusion, bf16[1,128,128,128]{3,2,1,0:T(8,128)(2,1)} %param.10), kind=kOutput, calls=%fused_computation.6 | convolution fusion | flops 1077936128 | bytes 29360256 | tf_op jit(solution)/shard_map/tji,tjd->tid/dot_general | solution.py:61
  107.0 17.7 %copy.13 = f32[128,256,128]{1,0,2:T(8,128)} copy(f32[128,256,128]{2,1,0:T(8,128)} %fusion.4) | data formatting | bytes 33554432 | tf_op jit(solution)/shard_map/tji,tjd->tid/dot_general | solution.py:61
  124.7 1.8 fusion.36
  126.5 0.0 all-reduce.2.cloned.1.call-update
  126.5 0.0 reduce-scatter.5.cloned.1.call-start
  126.6 10.8 %fusion.14 = bf16[8,128,256]{2,0,1:T(8,128)(2,1)S(1)} fusion(f32[128,256,128]{1,0,2:T(8,128)} %copy.13, f32[128]{0:T(128)S(1)} %compare_convert_fusion, s32[128]{0:T(128)S(1)} %bitcast.50), kind=kOutput, calls=%fused_computation.16 | convolution fusion | flops 402917376 | bytes 17302528 | tf_op jit(solution)/shard_map/tr,tid->rid/dot_general | solution.py:64
  137.4 0.9 copy.11
  138.3 0.0 reduce-scatter.5.cloned.1.call-update
  138.3 0.8 convolution_convert_fusion.1
  139.1 110.2 %all-reduce.2.cloned.1.call-done = f32[256,256]{1,0:T(8,128)} async-done(((f32[256,256]{1,0:T(8,128)}), f32[256,256]{1,0:T(8,128)}) %all-reduce.2.cloned.1.call-update) | async-done | bytes 262160 | tf_op jit(solution)/shard_map/psum | solution.py:58
  249.3 1.7 broadcast_multiply_fusion
  (24 shorter events, 0.1 us)
Async XLA Ops:
  8.0 0.9 copy-start
  8.0 116.7 %reduce-scatter.3.cloned.1.call-start = ((), (), s32[]{:S(2)}) async-start(), calls=%async_computation.2 | async-start | bytes 327680 | tf_op jit(solution)/shard_map/reduce_scatter | solution.py:34
  9.9 64.3 %collective-permute-start = (bf16[128,256]{1,0:T(8,128)(2,1)S(1)}, bf16[128,256]{1,0:T(8,128)(2,1)S(1)}, u32[]{:S(2)}, u32[]{:S(2)}) collective-permute-start(bf16[128,256]{1,0:T(8,128)(2,1)S(1)} %convolution_convert_fusion), channel_id=1, source_target_pairs={{0,1},{1,2},{2,3},{3,0},{4,5},{5,6},{6,7},{7,4},{8,9},{9,10},{10,1... | collective-permute-start | bytes 196616 | tf_op jit(solution)/shard_map/ppermute | solution.py:51
  44.9 17.7 %copy-start.3 = (s32[1,128]{1,0:T(1,128)S(1)}, s32[1,128]{1,0:T(1,128)}, u32[]{:S(2)}) copy-start(s32[1,128]{1,0:T(1,128)} %param.11) | copy-start | bytes 1540
  74.2 175.1 %all-reduce.2.cloned.1.call-start = ((), (), s32[]{:S(2)}) async-start(), calls=%async_computation.4 | async-start | bytes 524288 | tf_op jit(solution)/shard_map/psum | solution.py:58
  74.2 6.2 %collective-permute-start.1 = (bf16[128,256]{1,0:T(8,128)(2,1)S(1)}, bf16[128,256]{1,0:T(8,128)(2,1)S(1)}, u32[]{:S(2)}, u32[]{:S(2)}) collective-permute-start(bf16[128,256]{1,0:T(8,128)(2,1)S(1)} %collective-permute-done), channel_id=1, source_target_pairs={{0,1},{1,2},{2,3},{3,0},{4,5},{5,6},{6,7},{7,4},{8,9},{9,10},{10,1... | collective-permute-start | bytes 196616 | tf_op jit(solution)/shard_map/ppermute | solution.py:51
  80.5 7.0 %collective-permute-start.2 = (bf16[128,256]{1,0:T(8,128)(2,1)S(1)}, bf16[128,256]{1,0:T(8,128)(2,1)S(1)}, u32[]{:S(2)}, u32[]{:S(2)}) collective-permute-start(bf16[128,256]{1,0:T(8,128)(2,1)S(1)} %collective-permute-done.1), channel_id=1, source_target_pairs={{0,1},{1,2},{2,3},{3,0},{4,5},{5,6},{6,7},{7,4},{8,9},{9,10},{10,1... | collective-permute-start | bytes 196616 | tf_op jit(solution)/shard_map/ppermute | solution.py:51
  107.0 17.7 %copy-start.1 = (bf16[128,256]{1,0:T(8,128)(2,1)S(1)}, bf16[128,256]{1,0:T(8,128)(2,1)}, u32[]{:S(2)}) copy-start(bf16[128,256]{1,0:T(8,128)(2,1)} %param.8) | copy-start | bytes 196612
  107.0 19.6 %copy-start.4 = (s32[1,128]{1,0:T(1,128)S(1)}, s32[1,128]{1,0:T(1,128)}, u32[]{:S(2)}) copy-start(s32[1,128]{1,0:T(1,128)} %param.12) | copy-start | bytes 1540
  126.5 124.5 %reduce-scatter.5.cloned.1.call-start = ((), (), s32[]{:S(2)}) async-start(), calls=%async_computation.3 | async-start | bytes 589824 | tf_op jit(solution)/shard_map/reduce_scatter | solution.py:66
  126.5 11.8 %copy-start.2 = (bf16[128,256]{1,0:T(8,128)(2,1)S(1)}, bf16[128,256]{1,0:T(8,128)(2,1)}, u32[]{:S(2)}) copy-start(bf16[128,256]{1,0:T(8,128)(2,1)} %reduce-scatter.3.cloned.1.call-done) | copy-start | bytes 196612
Sparse Core Ops, SparseCore 0:
  74.3 19.1 reduce-scatter.2
  126.6 122.6 all-reduce.1
Sparse Core Ops, SparseCore 1:
  138.4 31.6 reduce-scatter.4
